TPU v7x, 256 devices: a whole 4x4x8 slice. The times are simulated.
256 devices in a mesh: section: 16 (over x_lo, y, core), dp: 16 (over z, x_hi).
Axes of the slice: x: 4 (x_hi: 2, x_lo: 2; x = x_hi * 2 + x_lo), y: 4, z: 8, core: 2. Of those that a mesh axis runs over, the one named last changes fastest.
Arguments:
- x_in: bfloat16 [64, 32, 8192], P('dp'), may hold values from -10 to 10
- segment_ids: int32 [64, 32], P('dp'), may hold values from 0 to 2, never falling along the last dimension, each value on 1 to 16 neighbouring positions
- norm_gain: bfloat16 [16, 8192], P('section'), may hold values from 0.5 to 1.5
- w_attn: bfloat16 [16, 8192, 512], P('section'), may hold values from -2 to 2
- final_gain: bfloat16 [8192], replicated, may hold values from 0.5 to 1.5
- upstream: bfloat16 [64, 32, 8192], P('dp'), may hold values from -6 to 6
Outputs:
- grad_attn: bfloat16 [16, 8192, 512], P('section', 'dp')
Inputs may be any that keep to these rules, and one draw needn't show every extreme that they name: `segment_ids`: segment numbers never fall along a row.
All inputs are finite; a program needn't handle non-finite values.
Results may differ from a plain program's by a relative error of at most 0.025.
Values may be sent and summed in bfloat16 or wider, within the bound.
No kernel may reach another device: no remote copies, remote signals or barrier semaphores. Data moves between devices by JAX's collectives and lax.ppermute only.
A program may use at most 128 MiB of HBM per device.

v0:
```python
import jax
import jax.numpy as jnp
from jax import lax
from jax.sharding import PartitionSpec as P

EPSILON = 1e-05
ROTARY_BASE = 500000.0


def passed_along(block, axis, distance):
    devices = range(lax.axis_size(axis))
    route = [((i - distance) % len(devices), i) for i in devices]
    return lax.ppermute(block, axis, route)


def normed(value_rows, gain):
    scale = lax.rsqrt(jnp.mean(value_rows * value_rows, axis=-1, keepdims=True) + EPSILON)
    return value_rows * scale * gain.astype(jnp.float32)


def tables(segs, head_size):
    length = segs.shape[1]
    index = jnp.arange(length, dtype=jnp.int32)
    earlier = jnp.sum((segs[:, None, :] < segs[:, :, None]).astype(jnp.int32), axis=-1)
    where_at = (index[None, :] - earlier).astype(jnp.float32)
    half = head_size // 2
    freq = ROTARY_BASE ** (-2.0 * jnp.arange(half, dtype=jnp.float32) / head_size)
    angle = where_at[..., None] * freq
    cosine = jnp.concatenate([jnp.cos(angle), jnp.cos(angle)], axis=-1)
    sine = jnp.concatenate([jnp.sin(angle), jnp.sin(angle)], axis=-1)
    allowed = (segs[:, :, None] == segs[:, None, :]) & (
        index[None, :, None] >= index[None, None, :]
    )
    return (cosine, sine, allowed)


def rotate(value_rows, cosine, sine):
    half = value_rows.shape[-1] // 2
    turned = jnp.concatenate([-value_rows[..., half:], value_rows[..., :half]], axis=-1)
    return value_rows * cosine + turned * sine


def attention(qkv, cosine, sine, allowed):
    head_size = qkv.shape[-1] // 3
    query_rows = rotate(qkv[..., :head_size], cosine, sine)
    key_rows = rotate(qkv[..., head_size : 2 * head_size], cosine, sine)
    value_rows = qkv[..., 2 * head_size :]
    attention_scores = jnp.einsum(
        "syt,sht->syh", query_rows, key_rows, precision=lax.Precision.HIGHEST
    ) * head_size ** (-0.5)
    attention_scores = jnp.where(allowed, attention_scores, -1e30)
    attention_probabilities = jax.nn.softmax(attention_scores, axis=-1)
    return jnp.einsum(
        "wom,wmz->woz", attention_probabilities, value_rows, precision=lax.Precision.HIGHEST
    )


def layer_forward(hidden_states, gain, weights, cosine, sine, allowed):
    head_size = weights.shape[1] // 4
    flat = hidden_states.astype(jnp.float32)
    xnorm = normed(flat, gain).astype(jnp.bfloat16)
    qkv = jnp.dot(xnorm, weights[:, : 3 * head_size], preferred_element_type=jnp.float32)
    heads = attention(qkv[None], cosine[None], sine[None], allowed[None])[0].astype(jnp.bfloat16)
    branch = lax.dot_general(
        heads,
        weights[:, 3 * head_size :],
        (((1,), (1,)), ((), ())),
        preferred_element_type=jnp.float32,
    )
    return (flat + branch).astype(jnp.bfloat16)


def layer_backward(hidden_states, grad_out, gain, weights, cosine, sine, allowed):
    head_size = weights.shape[1] // 4
    flat = hidden_states.astype(jnp.float32)
    xnorm = normed(flat, gain).astype(jnp.bfloat16)
    qkv = jnp.dot(xnorm, weights[:, : 3 * head_size], preferred_element_type=jnp.float32)
    heads32, pull = jax.vjp(
        lambda a: attention(a[None], cosine[None], sine[None], allowed[None])[0], qkv
    )
    heads = heads32.astype(jnp.bfloat16)
    grad_heads = jnp.dot(grad_out, weights[:, 3 * head_size :], preferred_element_type=jnp.float32)
    grad_qkv = pull(grad_heads)[0].astype(jnp.bfloat16)
    grad_norm = lax.dot_general(
        grad_qkv,
        weights[:, : 3 * head_size],
        (((1,), (1,)), ((), ())),
        preferred_element_type=jnp.float32,
    )
    _, norm_pull = jax.vjp(lambda a: normed(a, gain), flat)
    grad_in = (grad_out.astype(jnp.float32) + norm_pull(grad_norm)[0]).astype(jnp.bfloat16)
    return (grad_in, xnorm, grad_qkv, heads)


def head_backward(hidden_states, final_gain, cotangent):
    _, pull = jax.vjp(lambda a: normed(a, final_gain), hidden_states.astype(jnp.float32))
    return pull(cotangent.astype(jnp.float32))[0].astype(jnp.bfloat16)


def pick(stack, index):
    return lax.dynamic_index_in_dim(stack, index, 0, keepdims=False)


def place_into(stack, value, index, live):
    kept = jnp.where(live, value, pick(stack, index))
    return lax.dynamic_update_index_in_dim(stack, kept, index, 0)


def local(x_in, segment_ids, norm_gain, w_attn, final_gain, upstream):
    sections = lax.axis_size("section")
    place = lax.axis_index("section")
    micro_count, tok_count, width = x_in.shape
    head_size = w_attn.shape[2] // 4
    gain = norm_gain[0]
    weights = w_attn[0]
    cosine_all, sine_all, allowed_all = tables(segment_ids, head_size)
    head_section = 0
    steps = micro_count + sections
    empty = jnp.zeros((tok_count, width), jnp.bfloat16)

    def forward_step(turn, incoming, stash, grad_store):
        micro = turn - place
        live = (micro >= 0) & (micro < micro_count)
        slot = jnp.clip(micro, 0, micro_count - 1)
        source = jnp.where(place == 0, pick(x_in, slot), incoming)
        result = lax.cond(
            live,
            lambda a: layer_forward(
                a,
                gain,
                weights,
                pick(cosine_all, slot),
                pick(sine_all, slot),
                pick(allowed_all, slot),
            ),
            lambda a: a,
            source,
        )
        stash = place_into(stash, source, slot, live)
        head_micro = turn - sections
        head_live = (place == head_section) & (head_micro >= 0) & (head_micro < micro_count)
        head_slot = jnp.clip(head_micro, 0, micro_count - 1)
        grad = lax.cond(
            head_live,
            lambda a: head_backward(a, final_gain, pick(upstream, head_slot)),
            lambda a: a,
            incoming,
        )
        grad_store = place_into(grad_store, grad, head_slot, head_live)
        return (result, stash, grad_store)

    def forward_turn(turn, state):
        incoming = passed_along(state[0], "section", 1)
        return forward_step(turn, incoming, state[1], state[2])

    stack_zero = jnp.zeros((micro_count, tok_count, width), jnp.bfloat16)
    state = forward_step(0, empty, stack_zero, stack_zero)
    _, stash, grad_store = lax.fori_loop(1, steps, forward_turn, state)

    def backward_step(turn, incoming, saved):
        micro = turn - sections + place
        live = (micro >= 0) & (micro < micro_count)
        slot = jnp.clip(micro, 0, micro_count - 1)

        def active(a):
            return layer_backward(
                pick(stash, slot),
                a,
                gain,
                weights,
                pick(cosine_all, slot),
                pick(sine_all, slot),
                pick(allowed_all, slot),
            )

        def resting(a):
            return (
                a,
                jnp.zeros((tok_count, width), jnp.bfloat16),
                jnp.zeros((tok_count, 3 * head_size), jnp.bfloat16),
                jnp.zeros((tok_count, head_size), jnp.bfloat16),
            )

        grad_in, xnorm, grad_qkv, heads = lax.cond(live, active, resting, incoming)
        saved = (
            place_into(saved[0], xnorm, slot, live),
            place_into(saved[1], incoming, slot, live),
            place_into(saved[2], grad_qkv, slot, live),
            place_into(saved[3], heads, slot, live),
        )
        emit = (place == head_section) & (turn < micro_count)
        outgoing = jnp.where(emit, pick(grad_store, jnp.clip(turn, 0, micro_count - 1)), grad_in)
        return (outgoing, saved)

    def backward_turn(turn, state):
        incoming = passed_along(state[0], "section", -1)
        return backward_step(turn, incoming, state[1])

    saved = (
        stack_zero,
        stack_zero,
        jnp.zeros((micro_count, tok_count, 3 * head_size), jnp.bfloat16),
        jnp.zeros((micro_count, tok_count, head_size), jnp.bfloat16),
    )
    state = backward_step(0, empty, saved)
    _, saved = lax.fori_loop(1, steps, backward_turn, state)
    rows_all = micro_count * tok_count
    xnorm_flat = saved[0].reshape(rows_all, width)
    grad_flat = saved[1].reshape(rows_all, width)
    qkv_flat = saved[2].reshape(rows_all, 3 * head_size)
    heads_flat = saved[3].reshape(rows_all, head_size)
    left = lax.dot_general(
        xnorm_flat, qkv_flat, (((0,), (0,)), ((), ())), preferred_element_type=jnp.float32
    )
    right = lax.dot_general(
        grad_flat, heads_flat, (((0,), (0,)), ((), ())), preferred_element_type=jnp.float32
    )
    summed = lax.psum_scatter(
        jnp.concatenate([left, right], axis=1).astype(jnp.bfloat16),
        "dp",
        scatter_dimension=0,
        tiled=True,
    )
    return summed[None]


def solution(mesh):
    placed = (
        P("dp", None, None),
        P("dp", None),
        P("section", None),
        P("section", None, None),
        P(),
        P("dp", None, None),
    )
    return jax.shard_map(
        local, mesh=mesh, in_specs=placed, out_specs=P("section", "dp", None), check_vma=False
    )
```

profile of v0, /device:TPU:8, one launch (start us, length us, event | category | flops | bytes accessed | tf_op | source)
XLA Modules:
  0.0 1028.9 jit_solution(8104184390166656301)
XLA Ops:
  12.5 294.6 %while.48 = (s32[]{:T(128)}, bf16[32,8192]{1,0:T(8,128)(2,1)S(1)}, bf16[4,32,8192]{2,1,0:T(8,128)(2,1)S(1)}, bf16[4,32,8192]{2,1,0:T(8,128)(2,1)}, s32[]{:T(128)...) while((s32[]{:T(128)}, bf16[32,8192]{1,0:T(8,128)(2,1)S(1)}, ...), condition=%wide.region_16.17_spmd.clone, body=%wide.region_6.16_spmd.clone.sunk | while | flops 278987904 | bytes 24137160 | solution.py:158
  15.3 5.9 collective-permute-done
  27.2 13.6 %collective-permute-done = bf16[32,8192]{1,0:T(8,128)(2,1)S(1)} collective-permute-done((bf16[32,8192]{1,0:T(8,128)(2,1)S(1)}, bf16[32,8192]{1,0:T(8,128)(2,1)S(1)}, u32[]{:S(2)}, u32[]{:S(2)}) %collective-permute-start) | collective-permute-done | bytes 524320 | tf_op jit(solution)/shard_map/while/body/eval_jaxpr/ppermute | solution.py:13
  44.3 7.1 conditional.14
  54.3 8.0 collective-permute-done
  65.6 7.1 conditional.14
  75.6 8.0 collective-permute-done
  87.0 7.1 conditional.14
  97.0 8.0 collective-permute-done
  108.3 7.1 conditional.14
  118.3 5.9 collective-permute-done
  130.8 5.4 collective-permute-done
  142.3 5.9 collective-permute-done
  151.6 5.3 collective-permute-start
  163.6 5.3 collective-permute-start
  175.6 5.3 collective-permute-start
  187.6 5.3 collective-permute-start
  199.9 5.0 collective-permute-start
  219.6 5.1 collective-permute-done
  231.6 7.2 collective-permute-done
  245.0 8.0 collective-permute-done
  259.1 8.0 collective-permute-done
  273.2 13.5 %collective-permute-done = bf16[32,8192]{1,0:T(8,128)(2,1)S(1)} collective-permute-done((bf16[32,8192]{1,0:T(8,128)(2,1)S(1)}, bf16[32,8192]{1,0:T(8,128)(2,1)S(1)}, u32[]{:S(2)}, u32[]{:S(2)}) %collective-permute-start) | collective-permute-done | bytes 524320 | tf_op jit(solution)/shard_map/while/body/eval_jaxpr/ppermute | solution.py:13
  292.9 10.9 %collective-permute-done = bf16[32,8192]{1,0:T(8,128)(2,1)S(1)} collective-permute-done((bf16[32,8192]{1,0:T(8,128)(2,1)S(1)}, bf16[32,8192]{1,0:T(8,128)(2,1)S(1)}, u32[]{:S(2)}, u32[]{:S(2)}) %collective-permute-start) | collective-permute-done | bytes 524320 | tf_op jit(solution)/shard_map/while/body/eval_jaxpr/ppermute | solution.py:13
  311.5 460.6 %while.49 = (s32[]{:T(128)}, bf16[32,8192]{1,0:T(8,128)(2,1)}, bf16[4,32,8192]{2,1,0:T(8,128)(2,1)}, bf16[4,32,8192]{2,1,0:T(8,128)(2,1)}, bf16[4,32,384]{2,1,0:...) while((s32[]{:T(128)}, bf16[32,8192]{1,0:T(8,128)(2,1)}, ...), condition=%wide.region_32.33_spmd.clone, body=%wide.region_24.32_spmd.clone.sunk | while | flops 485137600 | bytes 65309304 | solution.py:206
  311.5 6.7 collective-permute-start.1
  321.2 4.0 collective-permute-done.1
  331.3 11.3 %collective-permute-start.1 = (bf16[32,8192]{1,0:T(8,128)(2,1)}, bf16[32,8192]{1,0:T(8,128)(2,1)S(1)}, u32[]{:S(2)}, u32[]{:S(2)}) collective-permute-start(bf16[32,8192]{1,0:T(8,128)(2,1)} %get-tuple-element.1550), channel_id=1, source_target_pairs={{16,0},{32,16},{48,32},{64,48},{80,64},{96,80},{112,96},{128,112},... | collective-permute-start | bytes 1572872 | tf_op jit(solution)/shard_map/while/body/eval_jaxpr/ppermute | solution.py:13
  345.5 4.0 collective-permute-done.1
  360.4 4.0 collective-permute-done.1
  370.4 13.4 %collective-permute-start.1 = (bf16[32,8192]{1,0:T(8,128)(2,1)}, bf16[32,8192]{1,0:T(8,128)(2,1)S(1)}, u32[]{:S(2)}, u32[]{:S(2)}) collective-permute-start(bf16[32,8192]{1,0:T(8,128)(2,1)} %get-tuple-element.1550), channel_id=1, source_target_pairs={{16,0},{32,16},{48,32},{64,48},{80,64},{96,80},{112,96},{128,112},... | collective-permute-start | bytes 1572872 | tf_op jit(solution)/shard_map/while/body/eval_jaxpr/ppermute | solution.py:13
  386.8 4.0 collective-permute-done.1
  396.8 15.3 %collective-permute-start.1 = (bf16[32,8192]{1,0:T(8,128)(2,1)}, bf16[32,8192]{1,0:T(8,128)(2,1)S(1)}, u32[]{:S(2)}, u32[]{:S(2)}) collective-permute-start(bf16[32,8192]{1,0:T(8,128)(2,1)} %get-tuple-element.1550), channel_id=1, source_target_pairs={{16,0},{32,16},{48,32},{64,48},{80,64},{96,80},{112,96},{128,112},... | collective-permute-start | bytes 1572872 | tf_op jit(solution)/shard_map/while/body/eval_jaxpr/ppermute | solution.py:13
  415.1 4.0 collective-permute-done.1
  425.2 15.5 %collective-permute-start.1 = (bf16[32,8192]{1,0:T(8,128)(2,1)}, bf16[32,8192]{1,0:T(8,128)(2,1)S(1)}, u32[]{:S(2)}, u32[]{:S(2)}) collective-permute-start(bf16[32,8192]{1,0:T(8,128)(2,1)} %get-tuple-element.1550), channel_id=1, source_target_pairs={{16,0},{32,16},{48,32},{64,48},{80,64},{96,80},{112,96},{128,112},... | collective-permute-start | bytes 1572872 | tf_op jit(solution)/shard_map/while/body/eval_jaxpr/ppermute | solution.py:13
  443.7 4.0 collective-permute-done.1
  453.7 15.4 %collective-permute-start.1 = (bf16[32,8192]{1,0:T(8,128)(2,1)}, bf16[32,8192]{1,0:T(8,128)(2,1)S(1)}, u32[]{:S(2)}, u32[]{:S(2)}) collective-permute-start(bf16[32,8192]{1,0:T(8,128)(2,1)} %get-tuple-element.1550), channel_id=1, source_target_pairs={{16,0},{32,16},{48,32},{64,48},{80,64},{96,80},{112,96},{128,112},... | collective-permute-start | bytes 1572872 | tf_op jit(solution)/shard_map/while/body/eval_jaxpr/ppermute | solution.py:13
  472.0 4.0 collective-permute-done.1
  482.1 4.0 collective-permute-start.1
  489.0 4.0 collective-permute-done.1
  506.0 4.0 collective-permute-done.1
  523.0 4.0 collective-permute-done.1
  533.0 4.0 collective-permute-start.1
  540.0 4.0 collective-permute-done.1
  557.0 4.0 collective-permute-done.1
  574.0 4.0 collective-permute-done.1
  590.9 38.8 %collective-permute-done.1 = bf16[32,8192]{1,0:T(8,128)(2,1)S(1)} collective-permute-done((bf16[32,8192]{1,0:T(8,128)(2,1)}, bf16[32,8192]{1,0:T(8,128)(2,1)S(1)}, u32[]{:S(2)}, u32[]{:S(2)}) %collective-permute-start.1) | collective-permute-done | bytes 524320 | tf_op jit(solution)/shard_map/while/body/eval_jaxpr/ppermute | solution.py:13
  629.7 12.9 %conditional.15 = (bf16[32,8192]{1,0:T(8,128)(2,1)}, bf16[32,8192]{1,0:T(8,128)(2,1)}, bf16[32,384]{1,0:T(8,128)(2,1)S(1)}, bf16[32,128]{1,0:T(8,128)(2,1)S(1)}) conditional(s32[]{:T(128)} %convert_element_type.230, bf16[32,8192]{1,0:T(8,128)(2,1)S(1)} %collective-permute-done.1, (bf16[32,8192]{1,0:T(8,128)(2,1)S(1)}, ...), branch_computations={%region_25.25_spmd, %region_26.31_spmd} | conditional | flops 484334784 | bytes 56231608 | solution.py:184
  633.1 4.5 fusion.119
  650.1 8.2 collective-permute-done.1
  658.3 12.9 %conditional.15 = (bf16[32,8192]{1,0:T(8,128)(2,1)}, bf16[32,8192]{1,0:T(8,128)(2,1)}, bf16[32,384]{1,0:T(8,128)(2,1)S(1)}, bf16[32,128]{1,0:T(8,128)(2,1)S(1)}) conditional(s32[]{:T(128)} %convert_element_type.230, bf16[32,8192]{1,0:T(8,128)(2,1)S(1)} %collective-permute-done.1, (bf16[32,8192]{1,0:T(8,128)(2,1)S(1)}, ...), branch_computations={%region_25.25_spmd, %region_26.31_spmd} | conditional | flops 484334784 | bytes 56231608 | solution.py:184
  661.7 4.5 fusion.119
  678.8 7.9 collective-permute-done.1
  686.7 12.9 %conditional.15 = (bf16[32,8192]{1,0:T(8,128)(2,1)}, bf16[32,8192]{1,0:T(8,128)(2,1)}, bf16[32,384]{1,0:T(8,128)(2,1)S(1)}, bf16[32,128]{1,0:T(8,128)(2,1)S(1)}) conditional(s32[]{:T(128)} %convert_element_type.230, bf16[32,8192]{1,0:T(8,128)(2,1)S(1)} %collective-permute-done.1, (bf16[32,8192]{1,0:T(8,128)(2,1)S(1)}, ...), branch_computations={%region_25.25_spmd, %region_26.31_spmd} | conditional | flops 484334784 | bytes 56231608 | solution.py:184
  690.0 4.5 fusion.119
  707.1 8.2 collective-permute-done.1
  715.3 12.9 %conditional.15 = (bf16[32,8192]{1,0:T(8,128)(2,1)}, bf16[32,8192]{1,0:T(8,128)(2,1)}, bf16[32,384]{1,0:T(8,128)(2,1)S(1)}, bf16[32,128]{1,0:T(8,128)(2,1)S(1)}) conditional(s32[]{:T(128)} %convert_element_type.230, bf16[32,8192]{1,0:T(8,128)(2,1)S(1)} %collective-permute-done.1, (bf16[32,8192]{1,0:T(8,128)(2,1)S(1)}, ...), branch_computations={%region_25.25_spmd, %region_26.31_spmd} | conditional | flops 484334784 | bytes 56231608 | solution.py:184
  718.6 4.5 fusion.119
  735.7 4.0 collective-permute-done.1
  745.8 13.2 %collective-permute-start.1 = (bf16[32,8192]{1,0:T(8,128)(2,1)}, bf16[32,8192]{1,0:T(8,128)(2,1)S(1)}, u32[]{:S(2)}, u32[]{:S(2)}) collective-permute-start(bf16[32,8192]{1,0:T(8,128)(2,1)} %get-tuple-element.1550), channel_id=1, source_target_pairs={{16,0},{32,16},{48,32},{64,48},{80,64},{96,80},{112,96},{128,112},... | collective-permute-start | bytes 1572872 | tf_op jit(solution)/shard_map/while/body/eval_jaxpr/ppermute | solution.py:13
  762.0 4.0 collective-permute-done.1
  775.9 4.5 bitcast_convert_fusion
  780.5 7.6 pad_maximum_fusion
  788.1 231.9 %reduce-scatter.2.cloned.1.call-done = bf16[512,512]{0,1:T(8,128)(2,1)} async-done(((bf16[8192,512]{0,1:T(8,128)(2,1)}), bf16[512,512]{0,1:T(8,128)(2,1)}) %reduce-scatter.2.cloned.1.call-update) | async-done | bytes 524304 | tf_op jit(solution)/shard_map/reduce_scatter | solution.py:218
  (604 shorter events, 415.4 us)
Async XLA Ops:
  6.5 1013.5 %reduce-scatter.2.cloned.1.call-start = ((), (), s32[]{:S(2)}) async-start(), calls=%async_computation.1 | async-start | bytes 8912896 | tf_op jit(solution)/shard_map/reduce_scatter | solution.py:218
  11.0 1.6 copy-start.10
  11.0 1.6 copy-start.13
  12.5 8.6 collective-permute-start
  21.2 0.8 copy-start.2
  24.6 16.3 %collective-permute-start = (bf16[32,8192]{1,0:T(8,128)(2,1)S(1)}, bf16[32,8192]{1,0:T(8,128)(2,1)S(1)}, u32[]{:S(2)}, u32[]{:S(2)}) collective-permute-start(bf16[32,8192]{1,0:T(8,128)(2,1)S(1)} %get-tuple-element.1481), channel_id=1, source_target_pairs={{240,0},{0,16},{16,32},{32,48},{48,64},{64,80},{80,96},{96,112},{1... | collective-permute-start | bytes 1572872 | tf_op jit(solution)/shard_map/while/body/eval_jaxpr/ppermute | solution.py:13
  51.4 10.8 %collective-permute-start = (bf16[32,8192]{1,0:T(8,128)(2,1)S(1)}, bf16[32,8192]{1,0:T(8,128)(2,1)S(1)}, u32[]{:S(2)}, u32[]{:S(2)}) collective-permute-start(bf16[32,8192]{1,0:T(8,128)(2,1)S(1)} %get-tuple-element.1481), channel_id=1, source_target_pairs={{240,0},{0,16},{16,32},{32,48},{48,64},{64,80},{80,96},{96,112},{1... | collective-permute-start | bytes 1572872 | tf_op jit(solution)/shard_map/while/body/eval_jaxpr/ppermute | solution.py:13
  62.3 0.8 copy-start.2
  72.8 10.8 %collective-permute-start = (bf16[32,8192]{1,0:T(8,128)(2,1)S(1)}, bf16[32,8192]{1,0:T(8,128)(2,1)S(1)}, u32[]{:S(2)}, u32[]{:S(2)}) collective-permute-start(bf16[32,8192]{1,0:T(8,128)(2,1)S(1)} %get-tuple-element.1481), channel_id=1, source_target_pairs={{240,0},{0,16},{16,32},{32,48},{48,64},{64,80},{80,96},{96,112},{1... | collective-permute-start | bytes 1572872 | tf_op jit(solution)/shard_map/while/body/eval_jaxpr/ppermute | solution.py:13
  83.6 0.8 copy-start.2
  94.2 10.8 %collective-permute-start = (bf16[32,8192]{1,0:T(8,128)(2,1)S(1)}, bf16[32,8192]{1,0:T(8,128)(2,1)S(1)}, u32[]{:S(2)}, u32[]{:S(2)}) collective-permute-start(bf16[32,8192]{1,0:T(8,128)(2,1)S(1)} %get-tuple-element.1481), channel_id=1, source_target_pairs={{240,0},{0,16},{16,32},{32,48},{48,64},{64,80},{80,96},{96,112},{1... | collective-permute-start | bytes 1572872 | tf_op jit(solution)/shard_map/while/body/eval_jaxpr/ppermute | solution.py:13
  105.0 0.8 copy-start.2
  115.5 8.7 collective-permute-start
  127.6 8.6 collective-permute-start
  136.2 0.8 copy-start.2
  139.6 8.6 collective-permute-start
  148.3 0.8 copy-start.2
  151.6 8.6 collective-permute-start
  160.3 0.8 copy-start.2
  163.6 8.6 collective-permute-start
  172.3 0.8 copy-start.2
  175.6 8.6 collective-permute-start
  187.6 8.9 collective-permute-start
  199.9 10.7 %collective-permute-start = (bf16[32,8192]{1,0:T(8,128)(2,1)S(1)}, bf16[32,8192]{1,0:T(8,128)(2,1)S(1)}, u32[]{:S(2)}, u32[]{:S(2)}) collective-permute-start(bf16[32,8192]{1,0:T(8,128)(2,1)S(1)} %get-tuple-element.1481), channel_id=1, source_target_pairs={{240,0},{0,16},{16,32},{32,48},{48,64},{64,80},{80,96},{96,112},{1... | collective-permute-start | bytes 1572872 | tf_op jit(solution)/shard_map/while/body/eval_jaxpr/ppermute | solution.py:13
  214.0 10.7 %collective-permute-start = (bf16[32,8192]{1,0:T(8,128)(2,1)S(1)}, bf16[32,8192]{1,0:T(8,128)(2,1)S(1)}, u32[]{:S(2)}, u32[]{:S(2)}) collective-permute-start(bf16[32,8192]{1,0:T(8,128)(2,1)S(1)} %get-tuple-element.1481), channel_id=1, source_target_pairs={{240,0},{0,16},{16,32},{32,48},{48,64},{64,80},{80,96},{96,112},{1... | collective-permute-start | bytes 1572872 | tf_op jit(solution)/shard_map/while/body/eval_jaxpr/ppermute | solution.py:13
  228.2 10.7 %collective-permute-start = (bf16[32,8192]{1,0:T(8,128)(2,1)S(1)}, bf16[32,8192]{1,0:T(8,128)(2,1)S(1)}, u32[]{:S(2)}, u32[]{:S(2)}) collective-permute-start(bf16[32,8192]{1,0:T(8,128)(2,1)S(1)} %get-tuple-element.1481), channel_id=1, source_target_pairs={{240,0},{0,16},{16,32},{32,48},{48,64},{64,80},{80,96},{96,112},{1... | collective-permute-start | bytes 1572872 | tf_op jit(solution)/shard_map/while/body/eval_jaxpr/ppermute | solution.py:13
  242.3 10.7 %collective-permute-start = (bf16[32,8192]{1,0:T(8,128)(2,1)S(1)}, bf16[32,8192]{1,0:T(8,128)(2,1)S(1)}, u32[]{:S(2)}, u32[]{:S(2)}) collective-permute-start(bf16[32,8192]{1,0:T(8,128)(2,1)S(1)} %get-tuple-element.1481), channel_id=1, source_target_pairs={{240,0},{0,16},{16,32},{32,48},{48,64},{64,80},{80,96},{96,112},{1... | collective-permute-start | bytes 1572872 | tf_op jit(solution)/shard_map/while/body/eval_jaxpr/ppermute | solution.py:13
  256.4 10.7 %collective-permute-start = (bf16[32,8192]{1,0:T(8,128)(2,1)S(1)}, bf16[32,8192]{1,0:T(8,128)(2,1)S(1)}, u32[]{:S(2)}, u32[]{:S(2)}) collective-permute-start(bf16[32,8192]{1,0:T(8,128)(2,1)S(1)} %get-tuple-element.1481), channel_id=1, source_target_pairs={{240,0},{0,16},{16,32},{32,48},{48,64},{64,80},{80,96},{96,112},{1... | collective-permute-start | bytes 1572872 | tf_op jit(solution)/shard_map/while/body/eval_jaxpr/ppermute | solution.py:13
  270.5 16.2 %collective-permute-start = (bf16[32,8192]{1,0:T(8,128)(2,1)S(1)}, bf16[32,8192]{1,0:T(8,128)(2,1)S(1)}, u32[]{:S(2)}, u32[]{:S(2)}) collective-permute-start(bf16[32,8192]{1,0:T(8,128)(2,1)S(1)} %get-tuple-element.1481), channel_id=1, source_target_pairs={{240,0},{0,16},{16,32},{32,48},{48,64},{64,80},{80,96},{96,112},{1... | collective-permute-start | bytes 1572872 | tf_op jit(solution)/shard_map/while/body/eval_jaxpr/ppermute | solution.py:13
  290.2 13.6 %collective-permute-start = (bf16[32,8192]{1,0:T(8,128)(2,1)S(1)}, bf16[32,8192]{1,0:T(8,128)(2,1)S(1)}, u32[]{:S(2)}, u32[]{:S(2)}) collective-permute-start(bf16[32,8192]{1,0:T(8,128)(2,1)S(1)} %get-tuple-element.1481), channel_id=1, source_target_pairs={{240,0},{0,16},{16,32},{32,48},{48,64},{64,80},{80,96},{96,112},{1... | collective-permute-start | bytes 1572872 | tf_op jit(solution)/shard_map/while/body/eval_jaxpr/ppermute | solution.py:13
  307.4 1.4 copy-start.3
  309.3 2.3 copy-start.4
  311.5 13.7 %collective-permute-start.1 = (bf16[32,8192]{1,0:T(8,128)(2,1)}, bf16[32,8192]{1,0:T(8,128)(2,1)S(1)}, u32[]{:S(2)}, u32[]{:S(2)}) collective-permute-start(bf16[32,8192]{1,0:T(8,128)(2,1)} %get-tuple-element.1550), channel_id=1, source_target_pairs={{16,0},{32,16},{48,32},{64,48},{80,64},{96,80},{112,96},{128,112},... | collective-permute-start | bytes 1572872 | tf_op jit(solution)/shard_map/while/body/eval_jaxpr/ppermute | solution.py:13
  331.3 18.3 %collective-permute-start.1 = (bf16[32,8192]{1,0:T(8,128)(2,1)}, bf16[32,8192]{1,0:T(8,128)(2,1)S(1)}, u32[]{:S(2)}, u32[]{:S(2)}) collective-permute-start(bf16[32,8192]{1,0:T(8,128)(2,1)} %get-tuple-element.1550), channel_id=1, source_target_pairs={{16,0},{32,16},{48,32},{64,48},{80,64},{96,80},{112,96},{128,112},... | collective-permute-start | bytes 1572872 | tf_op jit(solution)/shard_map/while/body/eval_jaxpr/ppermute | solution.py:13
  355.6 8.8 collective-permute-start.1
  370.4 20.4 %collective-permute-start.1 = (bf16[32,8192]{1,0:T(8,128)(2,1)}, bf16[32,8192]{1,0:T(8,128)(2,1)S(1)}, u32[]{:S(2)}, u32[]{:S(2)}) collective-permute-start(bf16[32,8192]{1,0:T(8,128)(2,1)} %get-tuple-element.1550), channel_id=1, source_target_pairs={{16,0},{32,16},{48,32},{64,48},{80,64},{96,80},{112,96},{128,112},... | collective-permute-start | bytes 1572872 | tf_op jit(solution)/shard_map/while/body/eval_jaxpr/ppermute | solution.py:13
  396.8 22.4 %collective-permute-start.1 = (bf16[32,8192]{1,0:T(8,128)(2,1)}, bf16[32,8192]{1,0:T(8,128)(2,1)S(1)}, u32[]{:S(2)}, u32[]{:S(2)}) collective-permute-start(bf16[32,8192]{1,0:T(8,128)(2,1)} %get-tuple-element.1550), channel_id=1, source_target_pairs={{16,0},{32,16},{48,32},{64,48},{80,64},{96,80},{112,96},{128,112},... | collective-permute-start | bytes 1572872 | tf_op jit(solution)/shard_map/while/body/eval_jaxpr/ppermute | solution.py:13
  425.2 22.5 %collective-permute-start.1 = (bf16[32,8192]{1,0:T(8,128)(2,1)}, bf16[32,8192]{1,0:T(8,128)(2,1)S(1)}, u32[]{:S(2)}, u32[]{:S(2)}) collective-permute-start(bf16[32,8192]{1,0:T(8,128)(2,1)} %get-tuple-element.1550), channel_id=1, source_target_pairs={{16,0},{32,16},{48,32},{64,48},{80,64},{96,80},{112,96},{128,112},... | collective-permute-start | bytes 1572872 | tf_op jit(solution)/shard_map/while/body/eval_jaxpr/ppermute | solution.py:13
  453.7 22.4 %collective-permute-start.1 = (bf16[32,8192]{1,0:T(8,128)(2,1)}, bf16[32,8192]{1,0:T(8,128)(2,1)S(1)}, u32[]{:S(2)}, u32[]{:S(2)}) collective-permute-start(bf16[32,8192]{1,0:T(8,128)(2,1)} %get-tuple-element.1550), channel_id=1, source_target_pairs={{16,0},{32,16},{48,32},{64,48},{80,64},{96,80},{112,96},{128,112},... | collective-permute-start | bytes 1572872 | tf_op jit(solution)/shard_map/while/body/eval_jaxpr/ppermute | solution.py:13
  482.1 11.0 %collective-permute-start.1 = (bf16[32,8192]{1,0:T(8,128)(2,1)}, bf16[32,8192]{1,0:T(8,128)(2,1)S(1)}, u32[]{:S(2)}, u32[]{:S(2)}) collective-permute-start(bf16[32,8192]{1,0:T(8,128)(2,1)} %get-tuple-element.1550), channel_id=1, source_target_pairs={{16,0},{32,16},{48,32},{64,48},{80,64},{96,80},{112,96},{128,112},... | collective-permute-start | bytes 1572872 | tf_op jit(solution)/shard_map/while/body/eval_jaxpr/ppermute | solution.py:13
  499.1 11.0 %collective-permute-start.1 = (bf16[32,8192]{1,0:T(8,128)(2,1)}, bf16[32,8192]{1,0:T(8,128)(2,1)S(1)}, u32[]{:S(2)}, u32[]{:S(2)}) collective-permute-start(bf16[32,8192]{1,0:T(8,128)(2,1)} %get-tuple-element.1550), channel_id=1, source_target_pairs={{16,0},{32,16},{48,32},{64,48},{80,64},{96,80},{112,96},{128,112},... | collective-permute-start | bytes 1572872 | tf_op jit(solution)/shard_map/while/body/eval_jaxpr/ppermute | solution.py:13
  516.1 11.0 %collective-permute-start.1 = (bf16[32,8192]{1,0:T(8,128)(2,1)}, bf16[32,8192]{1,0:T(8,128)(2,1)S(1)}, u32[]{:S(2)}, u32[]{:S(2)}) collective-permute-start(bf16[32,8192]{1,0:T(8,128)(2,1)} %get-tuple-element.1550), channel_id=1, source_target_pairs={{16,0},{32,16},{48,32},{64,48},{80,64},{96,80},{112,96},{128,112},... | collective-permute-start | bytes 1572872 | tf_op jit(solution)/shard_map/while/body/eval_jaxpr/ppermute | solution.py:13
  533.0 11.0 %collective-permute-start.1 = (bf16[32,8192]{1,0:T(8,128)(2,1)}, bf16[32,8192]{1,0:T(8,128)(2,1)S(1)}, u32[]{:S(2)}, u32[]{:S(2)}) collective-permute-start(bf16[32,8192]{1,0:T(8,128)(2,1)} %get-tuple-element.1550), channel_id=1, source_target_pairs={{16,0},{32,16},{48,32},{64,48},{80,64},{96,80},{112,96},{128,112},... | collective-permute-start | bytes 1572872 | tf_op jit(solution)/shard_map/while/body/eval_jaxpr/ppermute | solution.py:13
  550.1 11.0 %collective-permute-start.1 = (bf16[32,8192]{1,0:T(8,128)(2,1)}, bf16[32,8192]{1,0:T(8,128)(2,1)S(1)}, u32[]{:S(2)}, u32[]{:S(2)}) collective-permute-start(bf16[32,8192]{1,0:T(8,128)(2,1)} %get-tuple-element.1550), channel_id=1, source_target_pairs={{16,0},{32,16},{48,32},{64,48},{80,64},{96,80},{112,96},{128,112},... | collective-permute-start | bytes 1572872 | tf_op jit(solution)/shard_map/while/body/eval_jaxpr/ppermute | solution.py:13
  567.0 11.0 %collective-permute-start.1 = (bf16[32,8192]{1,0:T(8,128)(2,1)}, bf16[32,8192]{1,0:T(8,128)(2,1)S(1)}, u32[]{:S(2)}, u32[]{:S(2)}) collective-permute-start(bf16[32,8192]{1,0:T(8,128)(2,1)} %get-tuple-element.1550), channel_id=1, source_target_pairs={{16,0},{32,16},{48,32},{64,48},{80,64},{96,80},{112,96},{128,112},... | collective-permute-start | bytes 1572872 | tf_op jit(solution)/shard_map/while/body/eval_jaxpr/ppermute | solution.py:13
  584.0 45.7 %collective-permute-start.1 = (bf16[32,8192]{1,0:T(8,128)(2,1)}, bf16[32,8192]{1,0:T(8,128)(2,1)S(1)}, u32[]{:S(2)}, u32[]{:S(2)}) collective-permute-start(bf16[32,8192]{1,0:T(8,128)(2,1)} %get-tuple-element.1550), channel_id=1, source_target_pairs={{16,0},{32,16},{48,32},{64,48},{80,64},{96,80},{112,96},{128,112},... | collective-permute-start | bytes 1572872 | tf_op jit(solution)/shard_map/while/body/eval_jaxpr/ppermute | solution.py:13
  632.0 7.2 copy-start.1
  639.3 2.2 copy-start.6
  641.5 1.2 copy-start.7
  647.2 11.2 %collective-permute-start.1 = (bf16[32,8192]{1,0:T(8,128)(2,1)}, bf16[32,8192]{1,0:T(8,128)(2,1)S(1)}, u32[]{:S(2)}, u32[]{:S(2)}) collective-permute-start(bf16[32,8192]{1,0:T(8,128)(2,1)} %get-tuple-element.1550), channel_id=1, source_target_pairs={{16,0},{32,16},{48,32},{64,48},{80,64},{96,80},{112,96},{128,112},... | collective-permute-start | bytes 1572872 | tf_op jit(solution)/shard_map/while/body/eval_jaxpr/ppermute | solution.py:13
  660.7 7.2 copy-start.1
  667.9 2.2 copy-start.6
  670.1 1.2 copy-start.7
  675.8 10.9 %collective-permute-start.1 = (bf16[32,8192]{1,0:T(8,128)(2,1)}, bf16[32,8192]{1,0:T(8,128)(2,1)S(1)}, u32[]{:S(2)}, u32[]{:S(2)}) collective-permute-start(bf16[32,8192]{1,0:T(8,128)(2,1)} %get-tuple-element.1550), channel_id=1, source_target_pairs={{16,0},{32,16},{48,32},{64,48},{80,64},{96,80},{112,96},{128,112},... | collective-permute-start | bytes 1572872 | tf_op jit(solution)/shard_map/while/body/eval_jaxpr/ppermute | solution.py:13
  689.0 7.2 copy-start.1
  696.3 2.2 copy-start.6
  698.4 1.2 copy-start.7
  704.1 11.2 %collective-permute-start.1 = (bf16[32,8192]{1,0:T(8,128)(2,1)}, bf16[32,8192]{1,0:T(8,128)(2,1)S(1)}, u32[]{:S(2)}, u32[]{:S(2)}) collective-permute-start(bf16[32,8192]{1,0:T(8,128)(2,1)} %get-tuple-element.1550), channel_id=1, source_target_pairs={{16,0},{32,16},{48,32},{64,48},{80,64},{96,80},{112,96},{128,112},... | collective-permute-start | bytes 1572872 | tf_op jit(solution)/shard_map/while/body/eval_jaxpr/ppermute | solution.py:13
  717.6 7.2 copy-start.1
  724.9 2.2 copy-start.6
  727.0 1.2 copy-start.7
  732.7 7.0 collective-permute-start.1
  745.8 20.2 %collective-permute-start.1 = (bf16[32,8192]{1,0:T(8,128)(2,1)}, bf16[32,8192]{1,0:T(8,128)(2,1)S(1)}, u32[]{:S(2)}, u32[]{:S(2)}) collective-permute-start(bf16[32,8192]{1,0:T(8,128)(2,1)} %get-tuple-element.1550), channel_id=1, source_target_pairs={{16,0},{32,16},{48,32},{64,48},{80,64},{96,80},{112,96},{128,112},... | collective-permute-start | bytes 1572872 | tf_op jit(solution)/shard_map/while/body/eval_jaxpr/ppermute | solution.py:13
  772.1 3.8 copy-start.5
  (11 other events, 8.9 us)
Sparse Core Ops, SparseCore 0:
  788.3 231.7 reduce-scatter.1
where the time goes:
time: 1030 us
  waiting for transfers between devices  475 us (46%)
  other arithmetic  159 us (15%)
  local copies, waits for them, and re-layouts  154 us (15%)
  starting transfers between devices  151 us (15%)
  matrix products  75 us (7%)
  between operations  13.5 us (1%)
    ppermute x38, waiting for transfers between devices, passed_along(): return lax.ppermute(block, axis, route)  243 us
    reduce_scatter x1, waiting for transfers between devices, local(): lax.psum_scatter(jnp.concatenate([left, right], axis=1).astype(jnp.bfloat...  232 us
    ppermute x38, starting transfers between devices, passed_along(): return lax.ppermute(block, axis, route)  151 us
    dynamic_slice x122, local copies, waits for them, and re-layouts, pick(): return lax.dynamic_index_in_dim(stack, index, 0, keepdims=False)  108 us
    dynamic_update_slice x80, other arithmetic, place_into(): return lax.dynamic_update_index_in_dim(stack, kept, index, 0)  93.9 us
    select_n x20, other arithmetic, backward_step(): jnp.where(emit, pick(grad_store, jnp.clip(turn, 0, micro_count - 1)), gra...  41.4 us
  transfers between devices with their start and end apart: 39, of which 39 were waited for; matrix products, arithmetic and copies ran while one was open for 10% of the time, Pallas kernels for 0%

commit v1 on v0

v1 whole, which is shorter than its diff:
```python
import functools

import jax
import jax.numpy as jnp
from jax import lax
from jax.experimental import pallas as pl
from jax.experimental.pallas import tpu as pltpu
from jax.sharding import PartitionSpec as P

EPSILON = 1e-05
ROTARY_BASE = 500000.0
F32 = jnp.float32
BF16 = jnp.bfloat16
NN = (((1,), (0,)), ((), ()))
NT = (((1,), (1,)), ((), ()))
TN = (((0,), (0,)), ((), ()))


def mm(a, b, dims=NN):
    return lax.dot_general(a, b, dims, preferred_element_type=F32)


def split(a):
    high = a.astype(BF16)
    return high, (a - high.astype(F32)).astype(BF16)


def mm3(a, b, dims=NN):
    (ah, al), (bh, bl) = a, b
    return mm(ah, bh, dims) + (mm(al, bh, dims) + mm(ah, bl, dims))


def rowsum(a):
    return jnp.sum(a, axis=1, keepdims=True)


def scan_kernel(
    layers, width, hd,
    blocks, base, stats, cosine, sine, allowed,
    zo, final_scale,
    cols, diag, outs, grads, q_keep, k_keep, v_keep, p_keep, r_keep, s_keep, col_sem, diag_sem,
):
    first = [l * (l - 1) // 2 for l in range(layers + 1)]

    def copies(l):
        span = pl.ds(first[l], l)
        return (
            pltpu.make_async_copy(
                blocks.at[l, pl.ds(0, l)], cols.at[span, :, pl.ds(0, 2 * hd)], col_sem.at[0, l]
            ),
            pltpu.make_async_copy(
                blocks.at[pl.ds(0, l), l], cols.at[span, :, pl.ds(2 * hd, 2 * hd)], col_sem.at[1, l]
            ),
        )

    def diag_copy(l):
        return pltpu.make_async_copy(blocks.at[l, l, :, pl.ds(0, hd)], diag.at[l], diag_sem.at[l])

    diag_copy(0).start()
    for l in range(1, layers):
        for c in copies(l):
            c.start()
        diag_copy(l).start()

    def rope(u):
        return u * cosine[...] + pltpu.roll(u, hd // 2, 1) * sine[...]

    def rope_back(w):
        return w * cosine[...] - pltpu.roll(w, hd // 2, 1) * sine[...]

    scale = hd ** (-0.5)
    inv_width = 1.0 / width
    square = stats[:, 0:1]
    reach = stats[:, 1:2]
    for l in range(layers):
        if l:
            for c in copies(l):
                c.wait()
        diag_copy(l).wait()
        own = base[l]
        acc = jnp.concatenate(
            [
                own[:, : 2 * hd].astype(F32) + own[:, 2 * hd : 4 * hd].astype(F32),
                own[:, 4 * hd : 6 * hd].astype(F32),
            ],
            axis=1,
        )
        if l:
            rows = cols[pl.ds(first[l], l)].reshape(l * hd, 4 * hd)
            acc = acc + mm(outs[:, pl.ds(0, l * hd)], rows)
        s = lax.rsqrt(square * inv_width + EPSILON)
        q = rope(acc[:, :hd] * s)
        k = rope(acc[:, hd : 2 * hd] * s)
        v = acc[:, 2 * hd : 3 * hd] * s
        reached = acc[:, 3 * hd :]
        scores = mm3(split(q), split(k), NT) * scale
        scores = jnp.where(allowed[...] > 0.0, scores, -1e30)
        e = jnp.exp(scores - jnp.max(scores, axis=1, keepdims=True))
        p = e / rowsum(e)
        o = mm(p.astype(BF16), v.astype(BF16)).astype(BF16)
        outs[:, pl.ds(l * hd, hd)] = o
        zo[l, :, pl.ds(4 * hd, hd)] = o
        o32 = o.astype(F32)
        turned = mm(o, diag[l])
        square = square + rowsum(o32 * (2.0 * reached + turned))
        reach = reach + rowsum(o32 * own[:, 6 * hd :].astype(F32))
        q_keep[l] = q
        k_keep[l] = k
        v_keep[l] = v
        p_keep[l] = p
        r_keep[l] = reached + turned
        s_keep[l] = jnp.broadcast_to(s, (s.shape[0], hd))

    s_last = lax.rsqrt(square * inv_width + EPSILON)
    final_scale[...] = jnp.broadcast_to(s_last, final_scale.shape)
    back = s_last * s_last * s_last * inv_width * reach
    for l in range(layers):
        grads[:, pl.ds(l * hd, hd)] = s_last * base[l, :, pl.ds(6 * hd, hd)].astype(F32)

    for l in range(layers - 1, -1, -1):
        d_o = grads[:, pl.ds(l * hd, hd)] - back * r_keep[l]
        p, q, k, v, s = p_keep[l], q_keep[l], k_keep[l], v_keep[l], s_keep[l]
        d_o16 = d_o.astype(BF16)
        d_v = mm(p.astype(BF16), d_o16, TN)
        d_p = mm(d_o16, v.astype(BF16), NT)
        d_s = p * (d_p - rowsum(d_p * p)) * scale
        ds = split(d_s)
        d_q = mm3(ds, split(k))
        d_k = mm3(ds, split(q), TN)
        c = rowsum(d_q * q + d_k * k + d_v * v) * (s[:, 0:1] * s[:, 0:1]) * inv_width
        o32 = outs[:, pl.ds(l * hd, hd)].astype(F32)
        z = jnp.concatenate(
            [rope_back(d_q) * s, rope_back(d_k) * s, d_v * s, -(back * o32)], axis=1
        ).astype(BF16)
        zo[l, :, pl.ds(0, 4 * hd)] = z
        if l:
            rows = cols[pl.ds(first[l], l)].reshape(l * hd, 4 * hd)
            grads[:, pl.ds(0, l * hd)] += mm(z, rows, NT)
        back = back + c


def scan_layers(blocks, base, stats, cosine, sine, allowed, width):
    layers, _, hd, _ = blocks.shape
    rows = base.shape[1]
    vmem = pl.BlockSpec(memory_space=pltpu.VMEM)
    keep = pltpu.VMEM((layers, rows, hd), F32)
    return pl.pallas_call(
        functools.partial(scan_kernel, layers, width, hd),
        out_shape=(
            jax.ShapeDtypeStruct((layers, rows, 5 * hd), BF16),
            jax.ShapeDtypeStruct((rows, hd), F32),
        ),
        in_specs=[pl.BlockSpec(memory_space=pl.ANY)] + [vmem] * 5,
        out_specs=(vmem, vmem),
        scratch_shapes=[
            pltpu.VMEM((layers * (layers - 1) // 2, hd, 4 * hd), BF16),
            pltpu.VMEM((layers, hd, hd), BF16),
            pltpu.VMEM((rows, layers * hd), BF16),
            pltpu.VMEM((rows, layers * hd), F32),
            keep, keep, keep, keep, keep, keep,
            pltpu.SemaphoreType.DMA((2, layers)),
            pltpu.SemaphoreType.DMA((layers,)),
        ],
        compiler_params=pltpu.CompilerParams(vmem_limit_bytes=48 * 1024 * 1024),
        cost_estimate=pl.CostEstimate(
            flops=2 * 3 * layers * layers * rows * hd * 4 * hd,
            bytes_accessed=2 * layers * layers * hd * 2 * hd + 4 * layers * rows * 8 * hd,
            transcendentals=layers * rows * rows,
        ),
        name="scan_layers",
    )(blocks, base, stats, cosine, sine, allowed)


def swapped(block):
    n = lax.axis_size("section")
    return lax.ppermute(
        block, ("section", "dp"), [(a * n + b, b * n + a) for a in range(n) for b in range(n)]
    )


def partner(block):
    n = lax.axis_size("section")
    return lax.ppermute(block, "section", [(i, i ^ 1) for i in range(n)])


def all_of_dp(block):
    n = lax.axis_size("dp")
    return lax.all_to_all(jnp.broadcast_to(block[None], (n,) + block.shape), "dp", 0, 0)


def tables(segs, head_size):
    batch, length = segs.shape
    index = jnp.arange(length, dtype=jnp.int32)
    earlier = jnp.sum((segs[:, None, :] < segs[:, :, None]).astype(jnp.int32), axis=-1)
    where_at = (index[None, :] - earlier).astype(F32).reshape(batch * length)
    half = head_size // 2
    freq = ROTARY_BASE ** (-2.0 * jnp.arange(half, dtype=F32) / head_size)
    angle = where_at[:, None] * freq
    cosine, sine = jnp.cos(angle), jnp.sin(angle)
    flat = segs.reshape(batch * length)
    token = jnp.arange(batch * length, dtype=jnp.int32)
    allowed = (
        (flat[:, None] == flat[None, :])
        & (token[:, None] >= token[None, :])
        & (token[:, None] // length == token[None, :] // length)
    )
    return (
        jnp.concatenate([cosine, cosine], axis=-1),
        jnp.concatenate([-sine, sine], axis=-1),
        allowed.astype(F32),
    )


def three(a):
    high = a.astype(BF16)
    rest = a - high.astype(F32)
    middle = rest.astype(BF16)
    return [high, middle, (rest - middle.astype(F32)).astype(BF16)]


def local(x_in, segment_ids, norm_gain, w_attn, final_gain, upstream, scan=scan_layers):
    n = lax.axis_size("section")
    me = lax.axis_index("section")
    row = lax.axis_index("dp")
    micro_count, tok_count, width = x_in.shape
    rows = micro_count * tok_count
    part = width // n
    gain = norm_gain[0].astype(F32)
    weights = w_attn[0]
    hd = weights.shape[1] // 4
    w_in, w_out = weights[:, : 3 * hd], weights[:, 3 * hd :]
    x = x_in.reshape(rows, width)
    up = upstream.reshape(rows, width)
    x32, up32 = x.astype(F32), up.astype(F32)

    half = width // 2
    sent = lax.dynamic_slice_in_dim(w_out, (row % 2) * half, half, 0)
    mine = swapped(sent)
    other = partner(mine)
    odd = me % 2 == 1
    theirs = jnp.concatenate([jnp.where(odd, other, mine), jnp.where(odd, mine, other)], axis=0)

    w_scaled = jnp.concatenate(
        [w_in.astype(F32) * gain[:, None], w_out.astype(F32)], axis=1
    ).astype(BF16)
    tokens = jnp.concatenate(
        [
            lax.dynamic_slice_in_dim(x, me * part, part, 1),
            (lax.dynamic_slice_in_dim(up32, me * part, part, 1)
             * lax.dynamic_slice_in_dim(final_gain.astype(F32), me * part, part, 0)).astype(BF16),
        ],
        axis=0,
    )
    tokens = swapped(tokens)
    slices = lax.all_gather(
        jnp.concatenate([lax.dynamic_slice_in_dim(w_scaled, row * part, part, 0), tokens.reshape(-1, 4 * hd)], axis=0),
        "section",
    )

    up_gain = up32 * final_gain.astype(F32)
    first = mm((x32 * gain).astype(BF16), w_in)
    second = mm(jnp.concatenate([x, up_gain.astype(BF16)], axis=0), w_out)
    high, low = split(first[:, : 2 * hd])
    square = jnp.sum(x32 * x32, axis=1, keepdims=True)
    reach = jnp.sum(x32 * up_gain, axis=1, keepdims=True)
    segs = segment_ids.reshape(rows, 1).astype(BF16)
    extra = jnp.concatenate(
        three(square) + three(reach) + [segs, jnp.zeros((rows, hd - 7), BF16)], axis=1
    )
    packed = swapped(
        jnp.concatenate(
            [high, low, first[:, 2 * hd :].astype(BF16), second[:rows].astype(BF16),
             second[rows:].astype(BF16), extra],
            axis=1,
        )
    )
    base = all_of_dp(packed[:, : 7 * hd])
    extra = packed[:, 7 * hd :].astype(F32)
    stats = jnp.concatenate([rowsum(extra[:, :3]), rowsum(extra[:, 3:6])], axis=1)
    cosine, sine, allowed = tables(
        extra[:, 6].astype(jnp.int32).reshape(micro_count, tok_count), hd
    )

    block = jnp.concatenate(
        [mm((theirs.astype(F32) * gain[:, None]).astype(BF16), w_in, TN), mm(theirs, w_out, TN)],
        axis=1,
    ).astype(BF16)
    returned = swapped(block[:, 2 * hd :])
    on_diag = jnp.concatenate([block[:, 3 * hd :], jnp.zeros((hd, hd), BF16)], axis=1)
    shard = jnp.where(row < me, block[:, : 2 * hd], jnp.where(row == me, on_diag, returned))
    blocks = lax.all_gather(all_of_dp(shard), "section")

    zo, final_scale = scan(blocks, base, stats, cosine, sine, allowed, width)

    s_high, s_low = split(final_scale)
    pair_in = jnp.concatenate(
        [lax.dynamic_index_in_dim(zo, row, 0, keepdims=False),
         jnp.where(lax.broadcasted_iota(jnp.int32, s_high.shape, 1) < hd // 2, s_high, s_low)],
        axis=1,
    )
    pair = lax.all_gather(pair_in, "section").reshape(n * rows, 6 * hd)
    own = lax.all_to_all(zo, "section", 0, 0).reshape(n * rows, 5 * hd)
    z_own, o_own = own[:, : 4 * hd], own[:, 4 * hd :]
    z_pair, o_pair = pair[:, : 4 * hd], pair[:, 4 * hd : 5 * hd]
    below = row < me
    link = mm(jnp.where(below, o_pair, o_own), jnp.where(below, z_own, z_pair), TN).astype(BF16)
    links = all_of_dp(link)

    w_all = slices[:, :part]
    tokens_all = slices[:, part:].reshape(n, 2, rows, part)
    x_all = tokens_all[:, 0].reshape(n * rows, part)
    up_all = tokens_all[:, 1].reshape(n * rows, part)
    s_all = (
        pair[:, 5 * hd : 5 * hd + 1].astype(F32) + pair[:, 5 * hd + hd // 2 : 5 * hd + hd // 2 + 1].astype(F32)
    )
    index = lax.broadcasted_iota(jnp.int32, (n, 1, 1), 0)
    zero = jnp.zeros((), BF16)
    left_links = jnp.where(index < me, links, zero)
    column = lax.broadcasted_iota(jnp.int32, (1, 1, 4 * hd), 2)
    right_links = jnp.where(
        (index > me) | ((index == me) & (column >= 3 * hd)), links, zero
    )
    full = mm(x_all, z_own, TN) + lax.dot_general(
        w_all[:, :, 3 * hd :], left_links, (((0, 2), (0, 1)), ((), ())), preferred_element_type=F32
    )
    right = mm(up_all, (s_all * o_own.astype(F32)).astype(BF16), TN) + lax.dot_general(
        w_all, right_links, (((0, 2), (0, 2)), ((), ())), preferred_element_type=F32
    )
    gain_part = lax.dynamic_slice_in_dim(gain, row * part, part, 0)[:, None]
    return jnp.concatenate(
        [full[:, : 3 * hd] * gain_part, full[:, 3 * hd :] + right], axis=1
    ).astype(BF16)[None]


def solution(mesh):
    placed = (
        P("dp", None, None),
        P("dp", None),
        P("section", None),
        P("section", None, None),
        P(),
        P("dp", None, None),
    )
    return jax.shard_map(
        local, mesh=mesh, in_specs=placed, out_specs=P("section", "dp", None), check_vma=False
    )
```

time: 1030 us -> 561 us (0.54)
  waiting for transfers between devices: 475 us -> 291 us
  local copies, waits for them, and re-layouts: 154 us -> 14.8 us
  other arithmetic: 159 us -> 20.2 us
  starting transfers between devices: 151 us -> 41.8 us
  blocking collectives: 0 us -> 107 us
  matrix products: 75 us -> 30.3 us
  Pallas kernels: 0 us -> 35.1 us
    reduce_scatter x1 -> x0, waiting for transfers between devices: 232 us -> none  [local(): lax.psum_scatter(jnp.concatenate([left, right], axis=1).astype(jnp.bfloat...]
    ppermute x38 -> x5, starting transfers between devices: 151 us -> 21.4 us  [the longest x4 13.9 us: swapped(): lax.ppermute(block, ('section', 'dp'), [(a * n + b, b * n + a) for a in r...]
    ppermute x38 -> x5, waiting for transfers between devices: 243 us -> 133 us  [the longest x4 130 us: swapped(): lax.ppermute(block, ('section', 'dp'), [(a * n + b, b * n + a) for a in r...]
    all_to_all x0 -> x2, blocking collectives: none -> 107 us  [the longest x1 59.1 us: all_of_dp(): lax.all_to_all(jnp.broadcast_to(block[None], (n,) + block.shape), 'dp', 0...]
    dynamic_slice x122 -> x4, local copies, waits for them, and re-layouts: 108 us -> 1.08 us  [the longest x1 0.91 us: local(): lax.dynamic_slice_in_dim(x, me * part, part, 1)]
    dynamic_update_slice x80 -> x0, other arithmetic: 93.9 us -> none  [place_into(): return lax.dynamic_update_index_in_dim(stack, kept, index, 0)]
    all_gather x0 -> x3, waiting for transfers between devices: none -> 81.6 us  [the longest x1 80.2 us: local(): lax.all_gather(jnp.concatenate([lax.dynamic_slice_in_dim(w_scaled, row *...]
    all_to_all x0 -> x2, waiting for transfers between devices: none -> 76.8 us  [all_of_dp(): lax.all_to_all(jnp.broadcast_to(block[None], (n,) + block.shape), 'dp', 0...]
  transfers between devices with their start and end apart: 39 -> 10, of which waited for: 39 -> 9; matrix products, arithmetic and copies ran while one was open for 10% -> 8% of each run, Pallas kernels for 0% -> 0%
where the time goes in v1:
time: 561 us; the launch traced here: 555 us
  waiting for transfers between devices  291 us (52%)
  blocking collectives  107 us (19%)
  starting transfers between devices  41.8 us (7%)
  Pallas kernels  35.1 us (6%)
  matrix products  30.3 us (5%)
  other arithmetic  20.2 us (4%)
  local copies, waits for them, and re-layouts  14.8 us (3%)
  between operations  13.6 us (2%)
    ppermute x4, waiting for transfers between devices, swapped(): lax.ppermute(block, ('section', 'dp'), [(a * n + b, b * n + a) for a in r...  130 us
    all_gather x1, waiting for transfers between devices, local(): lax.all_gather(jnp.concatenate([lax.dynamic_slice_in_dim(w_scaled, row *...  80.2 us
    all_to_all x2, waiting for transfers between devices, all_of_dp(): lax.all_to_all(jnp.broadcast_to(block[None], (n,) + block.shape), 'dp', 0...  76.8 us
    all_to_all x1, blocking collectives, all_of_dp(): lax.all_to_all(jnp.broadcast_to(block[None], (n,) + block.shape), 'dp', 0...  59.1 us
    all_to_all x1, blocking collectives, local(): own = lax.all_to_all(zo, 'section', 0, 0).reshape(n * rows, 5 * hd)  48.4 us
    pallas_call x1, Pallas kernels, scan_layers(): pl.pallas_call(functools.partial(scan_kernel, layers, width, hd), out_sha...  35.1 us
    all_to_all x2, starting transfers between devices, all_of_dp(): lax.all_to_all(jnp.broadcast_to(block[None], (n,) + block.shape), 'dp', 0...  20.1 us
    dot_general x7, matrix products, mm(): return lax.dot_general(a, b, dims, preferred_element_type=F32)  19.2 us
  transfers between devices with their start and end apart: 10, of which 9 were waited for; matrix products, arithmetic and copies ran while one was open for 8% of the time, Pallas kernels for 0%

profile of v1, /device:TPU:8, one launch (start us, length us, event | category | flops | bytes accessed | tf_op | source)
XLA Modules:
  0.0 554.5 jit_solution(12727128446910213080)
XLA Ops:
  6.5 1.7 slice.114
  8.4 3.7 collective-permute-start.1
  12.1 97.9 %collective-permute-done.1 = bf16[4096,128]{1,0:T(8,128)(2,1)S(1)} collective-permute-done((bf16[4096,128]{1,0:T(8,128)(2,1)S(1)}, bf16[4096,128]{1,0:T(8,128)(2,1)S(1)}, u32[]{:S(2)}, u32[]{:S(2)}) %collective-permute-start.1) | collective-permute-done | bytes 1048608 | tf_op jit(solution)/shard_map/ppermute | solution.py:176
  110.0 7.5 %collective-permute-start.2 = (bf16[4096,128]{1,0:T(8,128)(2,1)S(1)}, bf16[4096,128]{1,0:T(8,128)(2,1)}, u32[]{:S(2)}, u32[]{:S(2)}) collective-permute-start(bf16[4096,128]{1,0:T(8,128)(2,1)S(1)} %collective-permute-done.1), channel_id=1, source_target_pairs={{0,16},{16,0},{32,48},{48,32},{64,80},{80,64},{96,112},{112,96},{1... | collective-permute-start | bytes 3145736 | tf_op jit(solution)/shard_map/ppermute | solution.py:183
  117.6 2.4 collective-permute-done.2
  119.9 1.5 broadcast_select_fusion.1
  121.5 2.6 fusion.51
  124.1 0.2 copy-done.1
  124.3 2.5 fusion.44
  126.8 3.6 collective-permute-start.3
  130.4 3.5 collective-permute-done.3
  133.9 0.1 broadcast_in_dim.26
  134.0 59.1 %all_to_all.20 = bf16[16,128,256]{2,1,0:T(8,128)(2,1)} all-to-all(bf16[16,128,256]{2,1,0:T(8,128)(2,1)S(1)} %broadcast_in_dim.26), channel_id=1, replica_groups=mesh['section'=16,'dp'=16] {'dp'}, dimensions={0} | all-to-all | bytes 2097152 | tf_op jit(solution)/shard_map/all_to_all | solution.py:188
  193.1 4.8 fusion.2
  198.0 1.2 fusion.7
  199.2 0.1 reduce_sum.50
  199.3 0.1 copy.65
  199.4 0.1 copy.66
  199.5 0.1 copy.67
  199.8 0.1 copy.68
  199.9 0.1 copy.69
  200.1 0.1 copy.70
  200.2 0.1 convert_element_type.336
  200.3 2.5 multiply_convert_fusion.1
  202.9 2.8 fusion.48
  205.8 0.2 concatenate.60
  205.9 1.9 collective-permute-start.4
  207.9 19.6 %collective-permute-done.4 = bf16[128,1024]{1,0:T(8,128)(2,1)S(1)} collective-permute-done((bf16[128,1024]{1,0:T(8,128)(2,1)S(1)}, bf16[128,1024]{1,0:T(8,128)(2,1)S(1)}, u32[]{:S(2)}, u32[]{:S(2)}) %collective-permute-start.4) | collective-permute-done | bytes 262176 | tf_op jit(solution)/shard_map/ppermute | solution.py:176
  227.5 2.4 broadcast_in_dim.28
  229.9 14.4 %all-to-all-start.1 = ((bf16[16,128,896]{2,1,0:T(8,128)(2,1)}), bf16[16,128,896]{2,1,0:T(8,128)(2,1)}, u32[]{:S(2)}, u32[]{:S(2)}) async-start(bf16[16,128,896]{2,1,0:T(8,128)(2,1)} %broadcast_in_dim.28), calls=%async_computation.1 | async-start | bytes 7340032 | tf_op jit(solution)/shard_map/all_to_all | solution.py:188
  244.3 0.2 all-gather.11.cloned.1.call-start
  244.6 0.2 fusion.61
  244.8 0.2 convert_reduce_fusion
  245.2 0.2 slice_reduce_fusion.1
  245.4 0.1 copy.72.stats
  245.5 0.3 fusion.66
  245.8 0.1 pad_maximum_fusion.10
  245.9 0.1 fusion.64.allowed
  246.0 76.8 %all-to-all-done.1.base = bf16[16,128,896]{2,1,0:T(8,128)(2,1)} async-done(((bf16[16,128,896]{2,1,0:T(8,128)(2,1)}), bf16[16,128,896]{2,1,0:T(8,128)(2,1)}, u32[]{:S(2)}, u32[]{:S(2)}) %all-to-all-start.1) | async-done | bytes 3670048 | tf_op jit(solution)/shard_map/all_to_all | solution.py:188
  322.8 1.2 all-gather.9.cloned.1.call-done
  324.0 35.1 %scan_layers.1 = (bf16[16,128,640]{2,1,0:T(8,128)(2,1)S(1)}, f32[128,128]{1,0:T(8,128)S(1)}) custom-call(bf16[16,16,128,256]{3,2,1,0:T(8,128)(2,1)} %bitcast.53, bf16[16,128,896]{2,1,0:T(8,128)(2,1)} %all-to-all-done.1.base, f32[128,2]{1,0:T(8,128)S(1)} %copy.72.stats, f32[128,128]{1,0:T(8,128)S(1)} %get-tuple-element.34.cosine, ...), custom_call_target="tpu_custom_call" | custom-call | flops 12884901888 | bytes 25165824 | tf_op jit(solution)/shard_map/scan_layers/pallas_call | solution.py:147
  359.2 0.7 pad_maximum_fusion.8
  360.1 0.9 constant_dynamic-slice_fusion.2
  361.0 1.0 multiply_convert_fusion.10
  362.0 4.7 collective-permute-start
  366.7 8.1 %multiply_convert_fusion = bf16[8192,384]{1,0:T(8,128)(2,1)} fusion(f32[8192]{0:T(1024)S(1)} %bitcast.49, bf16[8192,512]{1,0:T(8,128)(2,1)} %bitcast.33), kind=kLoop, calls=%fused_computation | loop fusion | flops 9437184 | bytes 12615680 | tf_op jit(solution)/shard_map/convert.11
  374.8 1.1 fusion.55
  375.9 9.3 %collective-permute-done = bf16[256,512]{1,0:T(8,128)(2,1)S(1)} collective-permute-done((bf16[256,512]{1,0:T(8,128)(2,1)S(1)}, bf16[256,512]{1,0:T(8,128)(2,1)S(1)}, u32[]{:S(2)}, u32[]{:S(2)}) %collective-permute-start) | collective-permute-done | bytes 262176 | tf_op jit(solution)/shard_map/ppermute | solution.py:176
  385.2 0.9 pad_maximum_fusion.5
  386.2 48.4 %all_to_all.21 = bf16[16,128,640]{2,1,0:T(8,128)(2,1)} all-to-all(bf16[16,128,640]{2,1,0:T(8,128)(2,1)S(1)} %get-tuple-element.7), channel_id=1, replica_groups=mesh['section'=16,'dp'=16] {'section'}, dimensions={0} | all-to-all | bytes 5242880 | tf_op jit(solution)/shard_map/all_to_all | solution.py:302
  434.6 0.2 all-gather.11.cloned.1.call-done
  434.7 3.2 fusion.43
  438.0 1.5 broadcast_in_dim.32
  439.5 5.8 %all-to-all-start.3 = ((bf16[16,128,512]{2,1,0:T(8,128)(2,1)}), bf16[16,128,512]{2,1,0:T(8,128)(2,1)}, u32[]{:S(2)}, u32[]{:S(2)}) async-start(bf16[16,128,512]{2,1,0:T(8,128)(2,1)} %broadcast_in_dim.32), calls=%async_computation.3 | async-start | bytes 4194304 | tf_op jit(solution)/shard_map/all_to_all | solution.py:188
  445.4 80.2 %all-gather.7.cloned.1.call-done = bf16[12288,512]{1,0:T(8,128)(2,1)} async-done(((bf16[768,512]{1,0:T(8,128)(2,1)}), bf16[12288,512]{1,0:T(8,128)(2,1)}) %all-gather.7.cloned.1.call-update) | async-done | bytes 12582928 | tf_op jit(solution)/shard_map/all_gather | solution.py:255
  525.6 2.6 slice.115
  528.2 1.7 fusion.76
  529.9 0.8 copy-done.3
  530.7 2.3 fusion.23
  533.0 1.7 add_reduce_fusion
  534.8 4.2 fusion.31
  539.1 6.9 %fusion.37 = f32[512,128]{0,1:T(8,128)S(1)} fusion(bf16[16,128,512]{2,1,0:T(8,128)(2,1)} %all-to-all-done.3, pred[16,512]{1,0:T(8,128)(4,1)S(1)} %and_or_fusion, bf16[16,768,512]{2,1,0:T(8,128)(2,1)} %bitcast.46), kind=kOutput, calls=%fused_computation.40 | convolution fusion | flops 1074790400 | bytes 10756096 | tf_op jit(solution)/shard_map/dot_general | solution.py:326
  546.1 0.9 fusion.47
  547.0 1.0 copy.74
  (57 shorter events, 1.0 us)
Async XLA Ops:
  6.5 317.5 %all-gather.9.cloned.1.call-start = ((), (), s32[]{:S(2)}) async-start(), calls=%async_computation.5 | async-start | bytes 17825792 | tf_op jit(solution)/shard_map/all_gather | solution.py:291
  6.5 111.0 %copy-start.7 = (bf16[1,8192]{1,0:T(2,128)(2,1)S(1)}, bf16[1,8192]{1,0:T(2,128)(2,1)}, u32[]{:S(2)}) copy-start(bf16[1,8192]{1,0:T(2,128)(2,1)} %param.8) | copy-start | bytes 49156
  8.3 113.2 %copy-start = (bf16[8192,128]{1,0:T(8,128)(2,1)}, bf16[8192,128]{1,0:T(8,128)(2,1)S(1)}, u32[]{:S(2)}) copy-start(bf16[8192,128]{1,0:T(8,128)(2,1)S(1)} %slice.114) | copy-start | bytes 6291460
  8.4 101.6 %collective-permute-start.1 = (bf16[4096,128]{1,0:T(8,128)(2,1)S(1)}, bf16[4096,128]{1,0:T(8,128)(2,1)S(1)}, u32[]{:S(2)}, u32[]{:S(2)}) collective-permute-start(bf16[4096,128]{1,0:T(8,128)(2,1)S(1)} %constant_dynamic-slice_fusion.1), channel_id=1, source_target_pairs={{0,0},{1,16},{2,32},{3,48},{4,64},{5,80},{6,96},{7,112},{8,128},{9... | collective-permute-start | bytes 3145736 | tf_op jit(solution)/shard_map/ppermute | solution.py:176
  110.0 9.9 %collective-permute-start.2 = (bf16[4096,128]{1,0:T(8,128)(2,1)S(1)}, bf16[4096,128]{1,0:T(8,128)(2,1)}, u32[]{:S(2)}, u32[]{:S(2)}) collective-permute-start(bf16[4096,128]{1,0:T(8,128)(2,1)S(1)} %collective-permute-done.1), channel_id=1, source_target_pairs={{0,16},{16,0},{32,48},{48,32},{64,80},{80,64},{96,112},{112,96},{1... | collective-permute-start | bytes 3145736 | tf_op jit(solution)/shard_map/ppermute | solution.py:183
  119.9 4.3 copy-start.1
  126.8 7.1 %collective-permute-start.3 = (bf16[128,256]{1,0:T(8,128)(2,1)S(1)}, bf16[128,256]{1,0:T(8,128)(2,1)S(1)}, u32[]{:S(2)}, u32[]{:S(2)}) collective-permute-start(bf16[128,256]{1,0:T(8,128)(2,1)S(1)} %pad_maximum_fusion.9), channel_id=1, source_target_pairs={{0,0},{1,16},{2,32},{3,48},{4,64},{5,80},{6,96},{7,112},{8,128},{9... | collective-permute-start | bytes 196616 | tf_op jit(solution)/shard_map/ppermute | solution.py:176
  193.1 4.9 copy-start.8
  193.1 4.9 copy-start.2
  193.1 4.9 copy-start.4
  198.0 2.2 copy-start.9
  200.3 2.6 copy-start.5
  205.9 21.5 %collective-permute-start.4 = (bf16[128,1024]{1,0:T(8,128)(2,1)S(1)}, bf16[128,1024]{1,0:T(8,128)(2,1)S(1)}, u32[]{:S(2)}, u32[]{:S(2)}) collective-permute-start(bf16[128,1024]{1,0:T(8,128)(2,1)S(1)} %concatenate.60), channel_id=1, source_target_pairs={{0,0},{1,16},{2,32},{3,48},{4,64},{5,80},{6,96},{7,112},{8,128},{9... | collective-permute-start | bytes 786440 | tf_op jit(solution)/shard_map/ppermute | solution.py:176
  229.9 92.9 %all-to-all-start.1 = ((bf16[16,128,896]{2,1,0:T(8,128)(2,1)}), bf16[16,128,896]{2,1,0:T(8,128)(2,1)}, u32[]{:S(2)}, u32[]{:S(2)}) async-start(bf16[16,128,896]{2,1,0:T(8,128)(2,1)} %broadcast_in_dim.28), calls=%async_computation.1 | async-start | bytes 7340032 | tf_op jit(solution)/shard_map/all_to_all | solution.py:188
  244.3 190.5 %all-gather.11.cloned.1.call-start = ((), (), s32[]{:S(2)}) async-start(), calls=%async_computation.6 | async-start | bytes 3342336 | tf_op jit(solution)/shard_map/all_gather | solution.py:301
  359.9 165.7 %all-gather.7.cloned.1.call-start = ((), (), s32[]{:S(2)}) async-start(), calls=%async_computation.4 | async-start | bytes 13369344 | tf_op jit(solution)/shard_map/all_gather | solution.py:255
  362.0 23.2 %collective-permute-start = (bf16[256,512]{1,0:T(8,128)(2,1)S(1)}, bf16[256,512]{1,0:T(8,128)(2,1)S(1)}, u32[]{:S(2)}, u32[]{:S(2)}) collective-permute-start(bf16[256,512]{1,0:T(8,128)(2,1)S(1)} %pad_maximum_fusion.7), channel_id=1, source_target_pairs={{0,0},{1,16},{2,32},{3,48},{4,64},{5,80},{6,96},{7,112},{8,128},{9... | collective-permute-start | bytes 786440 | tf_op jit(solution)/shard_map/ppermute | solution.py:176
  439.5 95.3 %all-to-all-start.3 = ((bf16[16,128,512]{2,1,0:T(8,128)(2,1)}), bf16[16,128,512]{2,1,0:T(8,128)(2,1)}, u32[]{:S(2)}, u32[]{:S(2)}) async-start(bf16[16,128,512]{2,1,0:T(8,128)(2,1)} %broadcast_in_dim.32), calls=%async_computation.3 | async-start | bytes 4194304 | tf_op jit(solution)/shard_map/all_to_all | solution.py:188
  528.2 2.5 copy-start.3
  539.1 7.0 %copy-start.6 = (bf16[16,1,128,512]{3,2,1,0:T(8,128)(2,1)S(1)}, bf16[16,1,128,512]{3,2,1,0:T(8,128)(2,1)}, u32[]{:S(2)}) copy-start(bf16[16,1,128,512]{3,2,1,0:T(8,128)(2,1)} %get-tuple-element.18) | copy-start | bytes 6291460
Sparse Core Ops, SparseCore 0:
  193.2 130.7 all-gather.8
  360.0 74.6 all-gather.10
  436.6 88.9 all-gather.6
